TPU v7x, 512 devices: a whole 4x8x8 slice. The times are simulated.
512 devices in a mesh: row: 16 (over y, core), col: 32 (over z, x).
Axes of the slice: x: 4, y: 8, z: 8, core: 2. Of those that a mesh axis runs over, the one named last changes fastest.
Arguments:
- points: float32 [96, 40960], P(None, ('row', 'col')), may hold values from -3 to 3
- scales: float32 [96], replicated, may hold values from 0.0001 to 1
- solution: float32 [97, 40960], P(None, ('row', 'col')), may hold values from -250 to 250
- residual: float32 [97, 40960], P(None, ('row', 'col')), may hold values from -250 to 250
- direction: float32 [97, 40960], P(None, ('row', 'col')), may hold values from -250 to 250
Outputs:
- solution_next: float32 [97, 40960], P(None, ('row', 'col'))
- residual_next: float32 [97, 40960], P(None, ('row', 'col'))
- direction_next: float32 [97, 40960], P(None, ('row', 'col'))
All inputs are finite; a program needn't handle non-finite values.
Results may differ from a plain program's by a relative error of at most 0.00018.
Values sent between devices are 32-bit elements; how exact they have to be, the bound alone decides.
A program may use at most 64 MiB of HBM per device.

v0:
```python
import jax
import jax.numpy as jnp
from jax import lax
from jax.sharding import PartitionSpec as P


def contract(left, right, dims):
    return lax.dot_general(
        left,
        right,
        (dims, ((), ())),
        precision=lax.Precision.HIGHEST,
        preferred_element_type=jnp.float32,
    )


def kernel_block(row_coords, col_coords, col_values, col_grads, col_square, col_proj):
    products = contract(row_coords, col_coords, ((0,), (0,)))
    row_square = jnp.sum(row_coords * row_coords, axis=0)
    kernel = jnp.exp(-0.5 * (row_square[:, None] + col_square[None, :] - 2.0 * products))
    slopes = contract(row_coords, col_grads, ((0,), (0,))) - col_proj[None, :]
    weighted = kernel * (col_values[None, :] + slopes)
    value_out = jnp.sum(weighted, axis=1)
    grad_out = (
        -row_coords * value_out[None, :]
        + contract(col_coords, weighted, ((1,), (1,)))
        + contract(col_grads, kernel, ((1,), (1,)))
    )
    return jnp.concatenate([value_out[None, :], grad_out], axis=0)


def partial_image(row_points, col_stack):
    design = row_points.shape[0]
    row_count = row_points.shape[1]
    col_coords = col_stack[:design]
    col_values = col_stack[design]
    col_grads = col_stack[design + 1 :]
    col_square = jnp.sum(col_coords * col_coords, axis=0)
    col_proj = jnp.sum(col_coords * col_grads, axis=0)
    block_rows = 512
    block_count = row_count // block_rows
    stacked = jnp.moveaxis(row_points.reshape(design, block_count, block_rows), 1, 0)

    def tile_rows(row_coords):
        return kernel_block(row_coords, col_coords, col_values, col_grads, col_square, col_proj)

    result = lax.map(tile_rows, stacked)
    return jnp.moveaxis(result, 0, 1).reshape(design + 1, row_count)


def body(points, scales, solution, residual, direction):
    scaled = points * jnp.sqrt(2.0 * scales)[:, None]
    moving = jnp.concatenate([scaled, direction], axis=0)
    row_points = lax.all_gather(scaled, "col", axis=1, tiled=True)
    col_stack = lax.all_gather(moving, "row", axis=1, tiled=True)
    image_field = lax.psum_scatter(
        partial_image(row_points, col_stack), "col", scatter_dimension=1, tiled=True
    )
    norm_old = lax.psum(jnp.sum(residual * residual), ("row", "col"))
    curvature = lax.psum(jnp.sum(direction * image_field), ("row", "col"))
    step_size = norm_old / curvature
    residual_next = residual - step_size * image_field
    norm_new = lax.psum(jnp.sum(residual_next * residual_next), ("row", "col"))
    solution_next = solution + step_size * direction
    direction_next = residual_next + norm_new / norm_old * direction
    return (solution_next, residual_next, direction_next)


def solution(mesh):
    return jax.shard_map(
        body,
        mesh=mesh,
        in_specs=(
            P(None, ("row", "col")),
            P(),
            P(None, ("row", "col")),
            P(None, ("row", "col")),
            P(None, ("row", "col")),
        ),
        out_specs=(P(None, ("row", "col")), P(None, ("row", "col")), P(None, ("row", "col"))),
        check_vma=False,
    )
```

profile of v0, /device:TPU:1, one launch (start us, length us, event | category | flops | bytes accessed | tf_op | source)
XLA Modules:
  0.0 594.1 jit_solution(1856177577569657160)
XLA Ops:
  8.7 45.7 %all_gather.6 = f32[96,2560]{0,1:T(8,128)S(1)} all-gather(f32[96,80]{0,1:T(8,128)S(1)} %broadcast_multiply_fusion), channel_id=1, replica_groups=mesh['row'=16,'col'=32] {'col'}, dimensions={1}, use_global_device_ids=true | all-gather | bytes 1013760 | tf_op jit(solution)/shard_map/all_gather | solution.py:54
  55.2 33.7 %all_gather.7 = f32[193,1280]{0,1:T(8,128)S(1)} all-gather(f32[193,80]{0,1:T(8,128)S(1)} %pad_maximum_fusion), channel_id=1, replica_groups=mesh['row'=16,'col'=32] {'row'}, dimensions={1}, use_global_device_ids=true | all-gather | bytes 1049920 | tf_op jit(solution)/shard_map/all_gather | solution.py:55
  89.9 1.1 slice.13
  91.4 1.3 copy.18
  92.8 1.3 copy.19
  95.1 76.7 %while.10 = (s32[]{:T(128)}, f32[5,97,512]{2,1,0:T(8,128)}, f32[5,96,512]{2,1,0:T(8,128)S(1)}, f32[1280]{0:T(1024)S(1)}, f32[96,1280]{1,0:T(8,128)S(1)}, /*index...) while((s32[]{:T(128)}, f32[5,97,512]{2,1,0:T(8,128)}, ...), condition=%wide.region_7.8_spmd, body=%wide.region_4.7_spmd.sunk | while | flops 3025485312 | bytes 26725592 | solution.py:47
  96.1 3.4 fusion.43
  99.5 2.7 convolution_bitcast_fusion.3
  102.2 3.8 fusion.44
  106.0 3.7 fusion.45
  111.4 3.4 fusion.43
  114.8 2.7 convolution_bitcast_fusion.3
  117.6 3.8 fusion.44
  121.3 3.7 fusion.45
  126.7 3.4 fusion.43
  130.2 2.7 convolution_bitcast_fusion.3
  132.9 3.8 fusion.44
  136.7 3.7 fusion.45
  142.1 3.4 fusion.43
  145.5 2.7 convolution_bitcast_fusion.3
  148.2 3.8 fusion.44
  152.0 3.7 fusion.45
  157.4 3.4 fusion.43
  160.8 2.7 convolution_bitcast_fusion.3
  163.6 3.8 fusion.44
  167.4 3.7 fusion.45
  171.8 2.8 copy.21
  175.2 209.9 %reduce-scatter.2.cloned.1.call-done = f32[97,80]{0,1:T(8,128)} async-done(((f32[97,2560]{0,1:T(8,128)}), f32[97,80]{0,1:T(8,128)}) %reduce-scatter.2.cloned.1.call-update) | async-done | bytes 31056 | tf_op jit(solution)/shard_map/reduce_scatter | solution.py:56
  385.1 1.4 multiply_reduce_fusion.3
  386.5 100.5 %all-reduce = (f32[]{:T(128)}, f32[]{:T(128)}) all-reduce(f32[]{:T(128)} %multiply_reduce_fusion.4, f32[]{:T(128)} %multiply_reduce_fusion.3), channel_id=1, replica_groups=mesh['row'=16,'col'=32] {'row','col'}, use_global_device_ids=true, to_apply=%region_1.0 | all-reduce | flops 2 | bytes 16 | tf_op jit(solution)/shard_map/psum | solution.py:59
  488.4 1.4 multiply_reduce_fusion.2
  489.8 95.5 %psum.23 = f32[]{:T(128)} all-reduce(f32[]{:T(128)} %get-tuple-element.82), channel_id=1, replica_groups=mesh['row'=16,'col'=32] {'row','col'}, use_global_device_ids=true, to_apply=%region_12.13 | all-reduce | flops 1 | bytes 8 | tf_op jit(solution)/shard_map/psum | solution.py:63
  (64 shorter events, 14.5 us)
Async XLA Ops:
  7.2 377.9 %reduce-scatter.2.cloned.1.call-start = ((), (), s32[]{:S(2)}) async-start(), calls=%async_computation.1 | async-start | bytes 1351680 | tf_op jit(solution)/shard_map/reduce_scatter | solution.py:56
  95.1 0.9 copy-start.1
  95.1 4.4 copy-start
  106.0 4.4 copy-start.2
  110.4 0.9 copy-start.1
  110.4 4.4 copy-start
  121.3 4.4 copy-start.2
  125.8 0.9 copy-start.1
  125.8 4.4 copy-start
  136.7 4.4 copy-start.2
  141.1 0.9 copy-start.1
  141.1 4.4 copy-start
  152.0 4.4 copy-start.2
  156.4 0.9 copy-start.1
  156.4 4.4 copy-start
  167.3 4.4 copy-start.2
  171.8 2.8 copy-start.4
  171.8 213.3 %copy-start.3 = (f32[97,80]{0,1:T(8,128)S(1)}, f32[97,80]{0,1:T(8,128)}, u32[]{:S(2)}) copy-start(f32[97,80]{0,1:T(8,128)} %param.11) | copy-start | bytes 93124
  171.8 414.9 %copy-start.6 = (f32[97,80]{0,1:T(8,128)S(1)}, f32[97,80]{0,1:T(8,128)}, u32[]{:S(2)}) copy-start(f32[97,80]{0,1:T(8,128)} %param.9) | copy-start | bytes 93124
  489.8 97.5 %copy-start.5 = (f32[97,80]{0,1:T(8,128)}, f32[97,80]{0,1:T(8,128)S(1)}, u32[]{:S(2)}) copy-start(f32[97,80]{0,1:T(8,128)S(1)} %get-tuple-element.83) | copy-start | bytes 93124
Sparse Core Ops, SparseCore 0:
  174.7 210.3 reduce-scatter.1
where the time goes:
time: 595 us; the launch traced here: 594 us
  blocking collectives  275 us (46%)
  waiting for transfers between devices  210 us (35%)
  matrix products  68 us (11%)
  between operations  16.8 us (3%)
  local copies, waits for them, and re-layouts  12.6 us (2%)
  other arithmetic  11.2 us (2%)
    reduce_scatter x1, waiting for transfers between devices, body(): lax.psum_scatter(partial_image(row_points, col_stack), 'col', scatter_dim...  210 us
    psum x1, blocking collectives, body(): norm_old = lax.psum(jnp.sum(residual * residual), ('row', 'col'))  101 us
    psum x1, blocking collectives, body(): norm_new = lax.psum(jnp.sum(residual_next * residual_next), ('row', 'col'))  95.5 us
    dot_general x20, matrix products, contract(): lax.dot_general(left, right, (dims, ((), ())), precision=lax.Precision.HI...  68 us
    all_gather x1, blocking collectives, body(): row_points = lax.all_gather(scaled, 'col', axis=1, tiled=True)  45.7 us
    all_gather x1, blocking collectives, body(): col_stack = lax.all_gather(moving, 'row', axis=1, tiled=True)  33.7 us
  transfers between devices with their start and end apart: 1, of which 1 were waited for; matrix products, arithmetic and copies ran while one was open for 0% of the time, Pallas kernels for 0%

commit v1 on v0

v1 whole, which is shorter than its diff:
```python
import functools
import math

import jax
import jax.numpy as jnp
from jax import lax
from jax.experimental import pallas as pl
from jax.experimental.pallas import tpu as pltpu
from jax.sharding import PartitionSpec as P

F32, BF16 = jnp.float32, jnp.bfloat16
MESH = pl.DeviceIdType.MESH
DESIGN = 96
LANES = 128
ROOT = math.sqrt(math.log2(math.e))
NT = (((1,), (1,)), ((), ()))
NN = (((1,), (0,)), ((), ()))
NORM, REST, ONE, ONE2 = 97, 98, 99, 100


def dot(a, b, dims):
    return lax.dot_general(a, b, dims, preferred_element_type=F32)


def split(x):
    high = x.astype(BF16)
    return high, (x - high.astype(F32)).astype(BF16)


def joined(x):
    high, low = split(x)
    return high.astype(F32) + low.astype(F32)


def rotate(index, shift, size):
    return lax.rem(index + shift, size)


def kernel(
    dims, block, tile,
    points_ref, scales_ref, solution_ref, residual_ref, direction_ref,
    solution_out, residual_out, direction_out,
    pad_p, pad_d, pad_r, rows, cols, stream,
    prod_hi, prod_lo, slope_hi, slope_lo, mix_w, mix_k,
    partial, from_x, group, from_z, vec, vec_in,
    zs_send, zs_recv, xs_send, xs_recv, ys_send, ys_recv, cs_send, cs_recv,
    xr_send, xr_recv, zr_send, zr_recv, v_send, v_recv,
):
    ny, nc, nz, nx = dims
    per_x = nz * block
    row, col = lax.axis_index("row"), lax.axis_index("col")
    y, core = row // nc, lax.rem(row, nc)
    z, x = col // nx, lax.rem(col, nx)

    def at_z(shift):
        return (row, rotate(z, shift, nz) * nx + x)

    def at_x(shift):
        return (row, z * nx + rotate(x, shift, nx))

    def at_y(shift):
        return (rotate(y, shift, ny) * nc + core, col)

    def at_cx(dc, dx):
        return (y * nc + rotate(core, dc, nc), z * nx + rotate(x, dx, nx))

    peers = [at_z(d) for d in range(1, nz)] + [at_y(d) for d in range(1, ny)]
    peers += [at_cx(c, d) for c in range(nc) for d in range(nx) if c or d]
    barrier = pltpu.get_barrier_semaphore()
    for peer in peers:
        pl.semaphore_signal(barrier, inc=1, device_id=peer, device_id_type=MESH)

    lane = lax.broadcasted_iota(jnp.int32, (LANES, LANES), 1)
    lane_b = lax.broadcasted_iota(jnp.int32, (block, LANES), 1)
    for pad in (pad_p, pad_d, pad_r):
        pad[...] = jnp.zeros_like(pad)
    pad_p[1 : DESIGN + 1, 0:block] = points_ref[...]
    pad_d[0 : DESIGN + 1, 0:block] = direction_ref[...]
    pad_r[0 : DESIGN + 1, 0:block] = residual_ref[...]
    inside = (lane_b >= 1) & (lane_b <= DESIGN)
    coords = pad_p[...].T[0:block] * (jnp.sqrt(2.0 * scales_ref[...]) * ROOT)
    coords = joined(coords)
    norm = -0.5 * jnp.sum(coords * coords, axis=1, keepdims=True)
    norm_main = joined(norm)
    own_row = jnp.where(inside, coords, 0.0)
    own_row = jnp.where(lane_b == NORM, norm_main, own_row)
    own_row = jnp.where(lane_b == REST, norm - norm_main, own_row)
    own_row = jnp.where((lane_b == ONE) | (lane_b == ONE2), 1.0, own_row)
    field = pad_d[...].T[0:block]
    grads = joined(jnp.where(inside, field * (1.0 / ROOT), 0.0))
    value = field[:, 0:1] - jnp.sum(coords * grads, axis=1, keepdims=True)
    value_main = joined(value)
    own_col = jnp.where(lane_b == ONE, value_main, grads)
    own_col = jnp.where(lane_b == ONE2, value - value_main, own_col)
    rows[0:block] = own_row
    cols[0, 0, 0:block] = own_row
    cols[0, 0, block:] = own_col

    pl.semaphore_wait(barrier, len(peers))

    def copy(src, dst, send, recv, peer):
        return pltpu.make_async_remote_copy(
            src_ref=src, dst_ref=dst, send_sem=send, recv_sem=recv, device_id=peer, device_id_type=MESH
        )

    def z_gather(d):
        return copy(
            rows.at[pl.ds(0, block)], rows.at[pl.ds(d * block, block)],
            zs_send.at[d], zs_recv.at[d], at_z(nz - d),
        )

    def y_gather(d):
        return copy(cols.at[0, 0], cols.at[0, d], ys_send.at[d], ys_recv.at[d], at_y(ny - d))

    def x_gather(d):
        return copy(
            rows.at[pl.ds(0, per_x)], rows.at[pl.ds(d * per_x, per_x)],
            xs_send.at[d], xs_recv.at[d], at_x(nx - d),
        )

    def c_gather(d):
        return copy(cols.at[0], cols.at[d], cs_send.at[d], cs_recv.at[d], at_cx(nc - d, 0))

    for d in range(1, nz):
        z_gather(d).start()
    for d in range(1, ny):
        y_gather(d).start()
    for d in range(1, nz):
        z_gather(d).wait_recv()
    for d in range(1, nx):
        x_gather(d).start()
    for d in range(1, ny):
        y_gather(d).wait_recv()
    for d in range(1, nc):
        c_gather(d).start()

    def factors(b, _):
        here = pl.ds(pl.multiple_of(b * block, block), block)
        sample = cols[b // ny, lax.rem(b, ny), 0:block]
        slope = cols[b // ny, lax.rem(b, ny), block:]
        other = jnp.where(lane_b < NORM, sample, pltpu.roll(sample, 2, 1))
        other = jnp.where((lane_b == NORM) | (lane_b == REST), 1.0, other)
        high, low = split(other)
        prod_hi[here, 0:LANES], prod_hi[here, LANES:] = high, high
        prod_lo[here, 0:LANES], prod_lo[here, LANES:] = low, low
        high, low = split(slope)
        slope_hi[here, 0:LANES], slope_hi[here, LANES:] = high, high
        slope_lo[here, 0:LANES], slope_lo[here, LANES:] = low, low
        high, low = split(jnp.where(lane_b == 0, 1.0, sample))
        mix_w[here, 0:LANES], mix_w[here, LANES:] = high, low
        high, low = split(slope * (ROOT * ROOT))
        mix_k[here, 0:LANES], mix_k[here, LANES:] = high, low
        return 0

    lax.fori_loop(0, ny, factors, 0)
    for d in range(1, nc):
        c_gather(d).wait_recv()
    lax.fori_loop(ny, ny * nc, factors, 0)
    for d in range(1, nx):
        x_gather(d).wait_recv()

    def x_reduce(k):
        return copy(partial.at[k], from_x.at[k], xr_send.at[k], xr_recv.at[k], at_x(k + 1))

    def step(k, _):
        high, low = split(rows[pl.ds(pl.multiple_of(rotate(k, 1, nx) * per_x, per_x), per_x)])
        stream[:, 0:LANES], stream[:, LANES:] = high, low
        left = stream[...]
        total = None
        for j in range(ny * nc * block // tile):
            c = pl.ds(j * tile, tile)
            weight = jnp.exp2(dot(left, prod_hi[c], NT) + dot(left, prod_lo[c], NT))
            slope = dot(left, slope_hi[c], NT) + dot(left, slope_lo[c], NT)
            weighted = weight * slope
            weight_hi, weight_lo = split(weight)
            weighted_hi, weighted_lo = split(weighted)
            term = dot(weighted_hi, mix_w[c], NN) + dot(weighted_lo, mix_w[c], NN)
            term = term + dot(weight_hi, mix_k[c], NN) + dot(weight_lo, mix_k[c], NN)
            total = term if total is None else total + term
        partial[k] = total[:, 0:LANES] + total[:, LANES:]

        @pl.when(k < nx - 1)
        def _():
            x_reduce(k).start()

        return 0

    lax.fori_loop(0, nx, step, 0)

    def z_reduce(d):
        return copy(group.at[d], from_z.at[d], zr_send.at[d], zr_recv.at[d], at_z(d))

    for k in range(nx - 1):
        x_reduce(k).wait_recv()
    for d in sorted(range(nz), key=lambda d: -min(d, nz - d)):
        here = pl.ds(d * block, block)
        total = partial[nx - 1, here]
        for k in range(nx - 1):
            total = total + from_x[k, here]
        group[d] = total
        if d:
            z_reduce(d).start()
    total = group[0]
    for d in range(1, nz):
        z_reduce(d).wait_recv()
        total = total + from_z[d]

    image = jnp.where(lane_b == 0, total, (total - rows[0:block] * total[:, 0:1]) * (1.0 / ROOT))
    pad_p[...] = jnp.zeros_like(pad_p)
    pad_p[0:block] = jnp.where(lane_b <= DESIGN, image, 0.0)
    image = pad_p[...].T
    residual, direction = pad_r[...], pad_d[...]

    def lanes_sum(a):
        return jnp.sum(a, axis=0, keepdims=True)

    sums = [lanes_sum(residual * residual), lanes_sum(direction * image), lanes_sum(residual * image), lanes_sum(image * image)]
    place = lax.broadcasted_iota(jnp.int32, (8, LANES), 0)
    sums = functools.reduce(lambda a, k: jnp.where(place == k, sums[k], a), range(4), jnp.zeros((8, LANES), F32))

    stages = [
        [at_z(d) for d in range(1, nz)],
        [at_cx(c, d) for c in range(nc) for d in range(nx) if c or d],
        [at_y(d) for d in range(1, ny)],
    ]
    for s, targets in enumerate(stages):
        vec[s] = sums
        copies = [
            copy(vec.at[s], vec_in.at[s, i], v_send.at[s, i], v_recv.at[s, i], peer) for i, peer in enumerate(targets)
        ]
        for c in copies:
            c.start()
        for i, c in enumerate(copies):
            c.wait_recv()
            sums = sums + vec_in[s, i]

    sums = jnp.sum(sums, axis=1, keepdims=True)
    norm_old, curvature, cross, square = (sums[k : k + 1] for k in range(4))
    step_size = norm_old / curvature
    norm_new = norm_old - 2.0 * step_size * cross + step_size * step_size * square
    ratio = norm_new / norm_old
    residual_next = residual - step_size * image
    direction_next = residual_next + ratio * direction
    solution_out[...] = solution_ref[...] + step_size * direction_ref[...]
    residual_out[...] = residual_next[0 : DESIGN + 1, 0:block]
    direction_out[...] = direction_next[0 : DESIGN + 1, 0:block]

    for d in range(1, nz):
        z_gather(d).wait_send()
        z_reduce(d).wait_send()
    for d in range(1, ny):
        y_gather(d).wait_send()
    for d in range(1, nx):
        x_gather(d).wait_send()
        x_reduce(d - 1).wait_send()
    for d in range(1, nc):
        c_gather(d).wait_send()
    for s, targets in enumerate(stages):
        for i, peer in enumerate(targets):
            copy(vec.at[s], vec_in.at[s, i], v_send.at[s, i], v_recv.at[s, i], peer).wait_send()


def build(dims, block, tile):
    ny, nc, nz, nx = dims
    width = ny * nc * block
    most = max(nz, ny, nc * nx)
    dma = pltpu.SemaphoreType.DMA
    vmem = pl.BlockSpec(memory_space=pltpu.VMEM)
    state = jax.ShapeDtypeStruct((DESIGN + 1, block), F32)

    def body(points, scales, solution, residual, direction):
        line = jnp.zeros((1, LANES), F32).at[0, 1 : DESIGN + 1].set(scales)
        return pl.pallas_call(
            functools.partial(kernel, dims, block, tile),
            out_shape=(state, state, state),
            in_specs=[vmem] * 5,
            out_specs=(vmem, vmem, vmem),
            scratch_shapes=[
                pltpu.VMEM((LANES, LANES), F32),
                pltpu.VMEM((LANES, LANES), F32),
                pltpu.VMEM((LANES, LANES), F32),
                pltpu.VMEM((nz * nx * block, LANES), F32),
                pltpu.VMEM((nc, ny, 2 * block, LANES), F32),
                pltpu.VMEM((nz * block, 2 * LANES), BF16),
                *[pltpu.VMEM((width, 2 * LANES), BF16) for _ in range(6)],
                pltpu.VMEM((nx, nz * block, LANES), F32),
                pltpu.VMEM((nx - 1, nz * block, LANES), F32),
                pltpu.VMEM((nz, block, LANES), F32),
                pltpu.VMEM((nz, block, LANES), F32),
                pltpu.VMEM((3, 8, LANES), F32),
                pltpu.VMEM((3, most, 8, LANES), F32),
                dma((nz,)), dma((nz,)), dma((nx,)), dma((nx,)), dma((ny,)), dma((ny,)), dma((nc,)), dma((nc,)),
                dma((nx,)), dma((nx,)), dma((nz,)), dma((nz,)), dma((3, most)), dma((3, most)),
            ],
            compiler_params=pltpu.CompilerParams(
                collective_id=0, has_side_effects=True, vmem_limit_bytes=48 * 2**20
            ),
            name="iteration",
        )(points, line, solution, residual, direction)

    return body


def solution(mesh, dims=None, block=80, tile=256):
    if dims is None:
        dims = (mesh.shape["row"] // 2, 2, mesh.shape["col"] // 4, 4)
    state = P(None, ("row", "col"))
    return jax.shard_map(
        build(dims, block, tile),
        mesh=mesh,
        in_specs=(state, P(), state, state, state),
        out_specs=(state, state, state),
        check_vma=False,
    )
```

time: 595 us -> 96.7 us (0.16)
  blocking collectives: 275 us -> 0 us
  waiting for transfers between devices: 210 us -> 0 us
  Pallas kernels: 0 us -> 88.2 us
  matrix products: 68 us -> 0 us
  between operations: 16.8 us -> 0.69 us
  other arithmetic: 11.2 us -> 1.29 us
  local copies, waits for them, and re-layouts: 12.6 us -> 6.12 us
    reduce_scatter x1 -> x0, waiting for transfers between devices: 210 us -> none  [body(): lax.psum_scatter(partial_image(row_points, col_stack), 'col', scatter_dim...]
    psum x2 -> x0, blocking collectives: 196 us -> none  [the longest x1 101 us: body(): norm_old = lax.psum(jnp.sum(residual * residual), ('row', 'col'))]
    pallas_call x0 -> x1, Pallas kernels: none -> 88.2 us  [body(): pl.pallas_call(functools.partial(kernel, dims, block, tile), out_shape=(s...]
    all_gather x2 -> x0, blocking collectives: 79.4 us -> none  [the longest x1 45.7 us: body(): row_points = lax.all_gather(scaled, 'col', axis=1, tiled=True)]
    dot_general x20 -> x0, matrix products: 68 us -> none  [contract(): lax.dot_general(left, right, (dims, ((), ())), precision=lax.Precision.HI...]
    while x34 -> x0, local copies, waits for them, and re-layouts: 8.72 us -> none
  transfers between devices with their start and end apart: 1 -> 0, of which waited for: 1 -> 0; matrix products, arithmetic and copies ran while one was open for 0% -> 0% of each run, Pallas kernels for 0% -> 0%
where the time goes in v1:
time: 96.7 us; the launch traced here: 96.4 us
  Pallas kernels  88.2 us (91%)
  local copies, waits for them, and re-layouts  6.12 us (6%)
  other arithmetic  1.29 us (1%)
    pallas_call x1, Pallas kernels, body(): pl.pallas_call(functools.partial(kernel, dims, block, tile), out_shape=(s...  88.2 us
    unnamed x12, local copies, waits for them, and re-layouts  2.53 us
    pallas_call x3, local copies, waits for them, and re-layouts, body(): pl.pallas_call(functools.partial(kernel, dims, block, tile), out_shape=(s...  2.12 us

profile of v1, /device:TPU:1, one launch (start us, length us, event | category | flops | bytes accessed | tf_op | source)
XLA Modules:
  0.0 96.4 jit_solution(197767164162256688)
XLA Ops:
  0.6 0.0 copy-start.3
  0.6 0.6 compare_reduce_fusion
  1.3 0.0 copy-done.3
  1.3 0.6 fusion
  2.0 0.6 slice.19
  2.5 0.9 scatter.4.scales_ref
  3.4 0.0 copy-start
  3.4 0.9 copy.8.points_ref
  4.3 0.0 copy-done
  4.3 0.0 copy-start.1
  4.3 0.1 copy.9.solution_ref
  4.4 0.7 copy-done.1
  5.1 0.0 copy-start.2
  5.1 0.1 copy.10.residual_ref
  5.2 0.7 copy-done.2
  5.9 0.1 copy.11.direction_ref
  6.0 88.2 %iteration.1 = (f32[97,80]{1,0:T(8,128)S(1)}, f32[97,80]{1,0:T(8,128)S(1)}, f32[97,80]{1,0:T(8,128)S(1)}) custom-call(f32[96,80]{1,0:T(8,128)S(1)} %copy.8.points_ref, f32[1,128]{1,0:T(1,128)S(1)} %scatter.4.scales_ref, f32[97,80]{1,0:T(8,128)S(1)} %copy.9.solution_ref, f32[97,80]{1,0:T(8,128)S(1)} %copy.10.residual_ref, f32[97,80]{1,0:T(8,128)S(1)} %copy.11.direction_ref), custom_call_target="tpu_custom_call" | custom-call | tf_op jit(solution)/shard_map/iteration/pallas_call | solution.py:273
  94.2 0.7 copy.12
  94.9 0.7 copy.13
  95.6 0.7 copy.14
  (2 shorter events, 0.0 us)
Async XLA Ops:
  0.6 0.7 copy-start.3
  3.4 0.9 copy-start
  4.3 0.8 copy-start.1
  5.1 0.8 copy-start.2

commit v2 on v0

v2 whole, which is shorter than its diff:
```python
import functools
import math

import jax
import jax.numpy as jnp
from jax import lax
from jax.experimental import pallas as pl
from jax.experimental.pallas import tpu as pltpu
from jax.sharding import PartitionSpec as P

F32, BF16 = jnp.float32, jnp.bfloat16
MESH = pl.DeviceIdType.MESH
DESIGN = 96
LANES = 128
ROOT = math.sqrt(math.log2(math.e))
NT = (((1,), (1,)), ((), ()))
NN = (((1,), (0,)), ((), ()))
NORM, REST, ONE, ONE2 = 97, 98, 99, 100


def dot(a, b, dims):
    return lax.dot_general(a, b, dims, preferred_element_type=F32)


def split(x):
    high = x.astype(BF16)
    return high, (x - high.astype(F32)).astype(BF16)


def joined(x):
    high, low = split(x)
    return high.astype(F32) + low.astype(F32)


def rotate(index, shift, size):
    return lax.rem(index + shift, size)


def ring(size):
    return sorted(range(size), key=lambda d: (min(d, size - d), d))


def wide(a, b):
    return jnp.concatenate([a, b], axis=1)


def kernel(
    dims, block, tile,
    points_hbm, scales_hbm, solution_hbm, residual_hbm, direction_hbm,
    solution_out, residual_out, direction_out,
    points_ref, scales_ref, solution_ref, residual_ref, direction_ref,
    pad, rows, cols, stream, coord_hi, coord_lo, slope_hi, slope_lo, grad_hi, grad_lo, pipe, acc,
    part, from_core, whole, from_y, vec, vec_in,
    load, z_send, z_recv, x_send, x_recv, y_send, y_recv, c_send, c_recv,
    yr_send, yr_recv, cr_send, cr_recv, v_send, v_recv,
):
    ny, nc, nz, nx = dims
    row, col = lax.axis_index("row"), lax.axis_index("col")
    y, core = row // nc, lax.rem(row, nc)
    z, x = col // nx, lax.rem(col, nx)
    ys, zs, xs = ring(ny), ring(nz), ring(nx)
    per = ny // 2
    half = nc * per * block
    items = 2 * nz * nx * block // tile

    def at_z(shift):
        return (row, rotate(z, shift, nz) * nx + x)

    def at_x(shift):
        return (row, z * nx + rotate(x, shift, nx))

    def at_y(shift):
        return (rotate(y, shift, ny) * nc + core, col)

    def at_cx(dc, dx):
        return (y * nc + rotate(core, dc, nc), z * nx + rotate(x, dx, nx))

    inputs = [
        (points_hbm, points_ref), (scales_hbm, scales_ref), (direction_hbm, direction_ref),
        (residual_hbm, residual_ref), (solution_hbm, solution_ref),
    ]
    loads = [pltpu.make_async_copy(src, dst, load.at[i]) for i, (src, dst) in enumerate(inputs)]
    for c in loads:
        c.start()

    peers = [at_z(d) for d in range(1, nz)] + [at_y(d) for d in range(1, ny)]
    peers += [at_cx(c, d) for c in range(nc) for d in range(nx) if c or d]
    barrier = pltpu.get_barrier_semaphore()
    for peer in peers:
        pl.semaphore_signal(barrier, inc=1, device_id=peer, device_id_type=MESH)

    lane = lax.broadcasted_iota(jnp.int32, (block, LANES), 1)
    for c in loads[:3]:
        c.wait()
    pad[...] = jnp.zeros_like(pad)
    pad[0, :, 1 : DESIGN + 1] = points_ref[...] * (jnp.sqrt(2.0 * scales_ref[...]) * ROOT)
    pad[1, :, 0 : DESIGN + 1] = direction_ref[...]
    coords = joined(pad[0])
    norm = -0.5 * jnp.sum(coords * coords, axis=1, keepdims=True)
    norm_main = joined(norm)
    norm_rest = norm - norm_main
    own_row = jnp.where(lane == NORM, norm_main, coords)
    own_row = jnp.where(lane == REST, norm_rest, own_row)
    own_row = jnp.where((lane == ONE) | (lane == ONE2), 1.0, own_row)
    own_col = jnp.where(lane == ONE, norm_main, coords)
    own_col = jnp.where(lane == ONE2, norm_rest, own_col)
    own_col = jnp.where((lane == NORM) | (lane == REST) | (lane == 0), 1.0, own_col)
    field = pad[1]
    grads = joined(jnp.where(lane >= 1, field * (1.0 / ROOT), 0.0))
    value = field[:, 0:1] - jnp.sum(coords * grads, axis=1, keepdims=True)
    value_main = joined(value)
    own_slope = jnp.where(lane == ONE, value_main, grads)
    own_slope = jnp.where(lane == ONE2, value - value_main, own_slope)
    rows[0, 0, 0:block] = own_row
    cols[0, 0:block] = own_col
    cols[0, block:] = own_slope

    pl.semaphore_wait(barrier, len(peers))

    def copy(src, dst, send, recv, peer):
        return pltpu.make_async_remote_copy(
            src_ref=src, dst_ref=dst, send_sem=send, recv_sem=recv, device_id=peer, device_id_type=MESH
        )

    def y_gather(r):
        h, k = divmod(r, per)
        there = rows.at[h, 0, pl.ds(k * block, block)]
        return copy(rows.at[0, 0, pl.ds(0, block)], there, y_send.at[r], y_recv.at[r], at_y(ny - ys[r]))

    def c_gather(h):
        return copy(rows.at[h, 0], rows.at[h, 1], c_send.at[h], c_recv.at[h], at_cx(1, 0))

    def z_gather(r):
        return copy(cols.at[0], cols.at[r * nx], z_send.at[r], z_recv.at[r], at_z(nz - zs[r]))

    def x_gather(r, i):
        here, there = cols.at[r * nx], cols.at[r * nx + i]
        return copy(here, there, x_send.at[r * nx + i], x_recv.at[r * nx + i], at_x(nx - xs[i]))

    def pass_on(r):
        if r:
            z_gather(r).wait_recv()
        for i in range(1, nx):
            x_gather(r, i).start()

    for r in range(1, max(ny, nz)):
        if r < ny:
            y_gather(r).start()
        if r < nz:
            z_gather(r).start()
        if r == 1:
            pass_on(0)
    acc[...] = jnp.zeros_like(acc)
    for c in loads[3:]:
        c.wait()
    residual, direction = residual_ref[...], direction_ref[...]

    def total_of(a):
        return jnp.sum(jnp.sum(a, axis=1, keepdims=True), axis=0, keepdims=True)

    norm_old = total_of(residual * residual)

    def factor(s, _):
        @pl.when(lax.rem(s, nx) > 0)
        def _():
            copy(cols.at[0], cols.at[s], x_send.at[s], x_recv.at[s], at_x(1)).wait_recv()

        here = pl.ds(pl.multiple_of(s * block, block), block)
        slope = cols[s, block:]
        coord_hi[here], coord_lo[here] = split(cols[s, 0:block])
        slope_hi[here], slope_lo[here] = split(slope)
        grad_hi[here], grad_lo[here] = split(slope * (ROOT * ROOT))
        return 0

    def rows_in(h):
        for r in range(h * per, (h + 1) * per):
            if r:
                y_gather(r).wait_recv()
        c_gather(h).start()
        c_gather(h).wait_recv()
        for c in range(nc):
            here = pl.ds(c * per * block, per * block)
            stream[h, here, 0:LANES], stream[h, here, LANES:] = split(rows[h, c])

    def place(n):
        def since(c):
            return (n + items - c) // items

        pair = since(2) - since(items // 2)
        far = since(items // 2) - since(4 * items // 5)
        last = since(4 * items // 5)
        h = pair * lax.rem(n, 2) + far
        t = (1 - since(2)) * n + pair * (n // 2 + 1 - 2 * lax.rem(n, 2))
        t = t + far * (n - 3 * items // 10) + last * (n - items // 2)
        fresh = (1 - h) * (1 - since(items // 2)) + since(3 * items // 5) - last
        return h, t, fresh

    def columns(t):
        return pl.ds(pl.multiple_of(t * tile, tile), tile)

    def first(n):
        h, t, fresh = place(n)
        low = (t * tile + block - 1) // block
        high = ((t + 1) * tile + block - 1) // block
        lax.fori_loop(low, low + fresh * (high - low), factor, 0)
        c, left = columns(t), stream[h]
        chi, clo, shi, slo = coord_hi[c], coord_lo[c], slope_hi[c], slope_lo[c]
        weight = jnp.exp2(dot(left, wide(chi, chi), NT) + dot(left, wide(clo, clo), NT))
        weighted = weight * (dot(left, wide(shi, shi), NT) + dot(left, wide(slo, slo), NT))
        return (*split(weighted), *split(weight))

    def second(n):
        h, t, _ = place(n)
        c, slot = columns(t), lax.rem(n, 2)
        by_coord, by_grad = wide(coord_hi[c], coord_lo[c]), wide(grad_hi[c], grad_lo[c])
        term = dot(pipe[slot, 0], by_coord, NN) + dot(pipe[slot, 1], by_coord, NN)
        term = term + dot(pipe[slot, 2], by_grad, NN) + dot(pipe[slot, 3], by_grad, NN)
        acc[h] = acc[h] + term

    def keep(n, values):
        slot = lax.rem(n, 2)
        for i, value in enumerate(values):
            pipe[slot, i] = value

    def c_reduce(h):
        return copy(part.at[h, 1], from_core.at[h], cr_send.at[h], cr_recv.at[h], at_cx(1, 0))

    def y_reduce(r):
        h, k = divmod(r, per)
        return copy(whole.at[h, pl.ds(k * block, block)], from_y.at[r], yr_send.at[r], yr_recv.at[r], at_y(ys[r]))

    def to_core(h):
        for c in range(nc):
            here = pl.ds(c * per * block, per * block)
            part[h, c] = acc[h, here, 0:LANES] + acc[h, here, LANES:]
        c_reduce(h).start()

    def to_y(h):
        c_reduce(h).wait_recv()
        whole[h] = part[h, 0] + from_core[h]
        for r in reversed(range(h * per, (h + 1) * per)):
            if r:
                y_reduce(r).start()

    def body(n, _):
        for at, ranks in events.items():

            @pl.when(n == at)
            def _(ranks=ranks):
                for r in ranks:
                    pass_on(r)

        @pl.when(n == 2)
        def _():
            rows_in(1)

        @pl.when(n == 4 * items // 5)
        def _():
            to_core(1)

        @pl.when(n == 4 * items // 5 + 1)
        def _():
            to_y(1)

        values = first(n + 1)
        second(n)
        keep(n + 1, values)
        return 0

    early = [r for r in (1, 2) if r < nz]
    events = {at: [r for r in ranks if r < nz] for at, ranks in EVENTS.items()}
    for r in early:
        pass_on(r)
    rows_in(0)
    keep(0, first(0))
    lax.fori_loop(0, items - 1, body, 0)
    second(items - 1)
    to_core(0)
    to_y(0)

    total = whole[0, 0:block]
    for r in range(1, ny):
        y_reduce(r).wait_recv()
        total = total + from_y[r]
    image = jnp.where(lane == 0, total, (total - own_row * total[:, 0:1]) * (1.0 / ROOT))[:, 0 : DESIGN + 1]

    sums = [norm_old, total_of(direction * image), total_of(residual * image), total_of(image * image)]
    spot = lax.broadcasted_iota(jnp.int32, (1, LANES), 1)
    line = jnp.zeros((1, LANES), F32)
    for k, value in enumerate(sums):
        line = jnp.where(spot == k, value, line)

    stages = [
        [at_z(d) for d in range(1, nz)],
        [at_cx(c, d) for c in range(nc) for d in range(nx) if c or d],
        [at_y(d) for d in range(1, ny)],
    ]
    exchanges = [
        [copy(vec.at[s], vec_in.at[s, i], v_send.at[s, i], v_recv.at[s, i], peer) for i, peer in enumerate(targets)]
        for s, targets in enumerate(stages)
    ]
    for s, copies in enumerate(exchanges):
        vec[s] = line
        for c in copies:
            c.start()
        for i, c in enumerate(copies):
            c.wait_recv()
            line = line + vec_in[s, i]

    norm_old, curvature, cross, square = (line[:, k : k + 1] for k in range(4))
    step_size = norm_old / curvature
    norm_new = norm_old - 2.0 * step_size * cross + step_size * step_size * square
    residual_next = residual - step_size * image
    solution_out[...] = solution_ref[...] + step_size * direction
    residual_out[...] = residual_next
    direction_out[...] = residual_next + norm_new / norm_old * direction

    for r in range(1, nz):
        z_gather(r).wait_send()
    for r in range(nz):
        for i in range(1, nx):
            x_gather(r, i).wait_send()
    for r in range(1, ny):
        y_gather(r).wait_send()
        y_reduce(r).wait_send()
    for h in range(2):
        c_gather(h).wait_send()
        c_reduce(h).wait_send()
    for copies in exchanges:
        for c in copies:
            c.wait_send()


EVENTS = {1: (3, 4), 6: (5, 6), 9: (7,)}


def build(dims, block, tile):
    ny, nc, nz, nx = dims
    width = nz * nx * block
    half = nc * ny * block // 2
    most = max(nz, ny, nc * nx)
    dma = pltpu.SemaphoreType.DMA
    vmem, hbm = pl.BlockSpec(memory_space=pltpu.VMEM), pl.BlockSpec(memory_space=pltpu.HBM)
    state = jax.ShapeDtypeStruct((block, DESIGN + 1), F32)
    inputs = [(block, DESIGN), (1, DESIGN)] + [(block, DESIGN + 1)] * 3

    def body(points, scales, solution, residual, direction):
        outs = pl.pallas_call(
            functools.partial(kernel, dims, block, tile),
            out_shape=(state, state, state),
            in_specs=[hbm] * 5,
            out_specs=(vmem, vmem, vmem),
            scratch_shapes=[
                *[pltpu.VMEM(shape, F32) for shape in inputs],
                pltpu.VMEM((2, block, LANES), F32),
                pltpu.VMEM((2, nc, ny // 2 * block, LANES), F32),
                pltpu.VMEM((nz * nx, 2 * block, LANES), F32),
                pltpu.VMEM((2, half, 2 * LANES), BF16),
                *[pltpu.VMEM((width, LANES), BF16) for _ in range(6)],
                pltpu.VMEM((2, 4, half, tile), BF16),
                pltpu.VMEM((2, half, 2 * LANES), F32),
                pltpu.VMEM((2, nc, ny // 2 * block, LANES), F32),
                pltpu.VMEM((2, ny // 2 * block, LANES), F32),
                pltpu.VMEM((2, ny // 2 * block, LANES), F32),
                pltpu.VMEM((ny, block, LANES), F32),
                pltpu.VMEM((3, 1, LANES), F32),
                pltpu.VMEM((3, most, 1, LANES), F32),
                dma((5,)), dma((nz,)), dma((nz,)), dma((nz * nx,)), dma((nz * nx,)), dma((ny,)), dma((ny,)),
                dma((2,)), dma((2,)), dma((ny,)), dma((ny,)), dma((2,)), dma((2,)), dma((3, most)), dma((3, most)),
            ],
            compiler_params=pltpu.CompilerParams(
                collective_id=0, has_side_effects=True, vmem_limit_bytes=48 * 2**20
            ),
            name="iteration",
        )(points.T, scales.reshape(1, DESIGN), solution.T, residual.T, direction.T)
        return tuple(o.T for o in outs)

    return body


def solution(mesh, dims=None, block=80, tile=256):
    if dims is None:
        dims = (mesh.shape["row"] // 2, 2, mesh.shape["col"] // 4, 4)
    state = P(None, ("row", "col"))
    return jax.shard_map(
        build(dims, block, tile),
        mesh=mesh,
        in_specs=(state, P(), state, state, state),
        out_specs=(state, state, state),
        check_vma=False,
    )
```

time: 595 us -> 81.2 us (0.14)
  blocking collectives: 275 us -> 0 us
  waiting for transfers between devices: 210 us -> 0 us
  Pallas kernels: 0 us -> 74.6 us
  matrix products: 68 us -> 0 us
  between operations: 16.8 us -> 0.65 us
  other arithmetic: 11.2 us -> 0 us
  local copies, waits for them, and re-layouts: 12.6 us -> 5.61 us
    reduce_scatter x1 -> x0, waiting for transfers between devices: 210 us -> none  [body(): lax.psum_scatter(partial_image(row_points, col_stack), 'col', scatter_dim...]
    psum x2 -> x0, blocking collectives: 196 us -> none  [the longest x1 101 us: body(): norm_old = lax.psum(jnp.sum(residual * residual), ('row', 'col'))]
    all_gather x2 -> x0, blocking collectives: 79.4 us -> none  [the longest x1 45.7 us: body(): row_points = lax.all_gather(scaled, 'col', axis=1, tiled=True)]
    pallas_call x0 -> x1, Pallas kernels: none -> 74.6 us  [body(): pl.pallas_call(functools.partial(kernel, dims, block, tile), out_shape=(s...]
    dot_general x20 -> x0, matrix products: 68 us -> none  [contract(): lax.dot_general(left, right, (dims, ((), ())), precision=lax.Precision.HI...]
    while x34 -> x0, local copies, waits for them, and re-layouts: 8.72 us -> none
  transfers between devices with their start and end apart: 1 -> 0, of which waited for: 1 -> 0; matrix products, arithmetic and copies ran while one was open for 0% -> 0% of each run, Pallas kernels for 0% -> 0%
where the time goes in v2:
time: 81.2 us; the launch traced here: 80.8 us
  Pallas kernels  74.6 us (92%)
  local copies, waits for them, and re-layouts  5.61 us (7%)
    pallas_call x1, Pallas kernels, body(): pl.pallas_call(functools.partial(kernel, dims, block, tile), out_shape=(s...  74.6 us
    unnamed x13, local copies, waits for them, and re-layouts  5.61 us

profile of v2, /device:TPU:1, one launch (start us, length us, event | category | flops | bytes accessed | tf_op | source)
XLA Modules:
  0.0 80.8 jit_solution(18074004818337430494)
XLA Ops:
  0.6 0.0 copy-start.4
  0.6 0.6 copy-done.4
  1.3 0.0 copy-start
  1.3 0.8 copy-done
  2.1 0.0 copy-start.1
  2.1 0.8 copy-done.1
  2.8 0.0 copy-start.2
  2.8 0.8 copy-done.2
  3.6 0.0 copy-start.3
  3.6 0.8 copy-done.3
  4.4 74.6 %iteration.1 = (f32[80,97]{1,0:T(8,128)S(1)}, f32[80,97]{1,0:T(8,128)S(1)}, f32[80,97]{1,0:T(8,128)S(1)}) custom-call(f32[80,96]{1,0:T(8,128)S(1)} %bitcast.8, f32[1,96]{1,0:T(1,128)S(1)} %bitcast.15, f32[80,97]{1,0:T(8,128)S(1)} %bitcast.9, f32[80,97]{1,0:T(8,128)S(1)} %bitcast.10, f32[80,97]{1,0:T(8,128)S(1)} %bitcast.11), custom_call_target="tpu_custom_call" | custom-call | tf_op jit(solution)/shard_map/iteration/pallas_call | solution.py:348
  79.0 0.6 copy.11
  79.6 0.6 copy.12
  80.2 0.6 copy.13
Async XLA Ops:
  0.6 0.7 copy-start.4
  1.3 0.8 copy-start
  2.1 0.8 copy-start.1
  2.8 0.8 copy-start.2
  3.6 0.8 copy-start.3

commit v3 on v2

--- a/solution.py
+++ b/solution.py
@@ -186,13 +186,13 @@
         def since(c):
             return (n + items - c) // items
 
-        pair = since(2) - since(items // 2)
-        far = since(items // 2) - since(4 * items // 5)
-        last = since(4 * items // 5)
+        pair = since(2) - since(2 + 2 * PAIRS)
+        last = since(2 + PAIRS + items // 2)
+        far = since(2 + 2 * PAIRS) - last
         h = pair * lax.rem(n, 2) + far
         t = (1 - since(2)) * n + pair * (n // 2 + 1 - 2 * lax.rem(n, 2))
-        t = t + far * (n - 3 * items // 10) + last * (n - items // 2)
-        fresh = (1 - h) * (1 - since(items // 2)) + since(3 * items // 5) - last
+        t = t + far * (n - 2 - PAIRS) + last * (n - items // 2)
+        fresh = (1 - h) * (1 - last) + since(4 + 2 * PAIRS) - last
         return h, t, fresh
 
     def columns(t):
@@ -254,11 +254,11 @@
         def _():
             rows_in(1)
 
-        @pl.when(n == 4 * items // 5)
+        @pl.when(n == 2 + PAIRS + items // 2)
         def _():
             to_core(1)
 
-        @pl.when(n == 4 * items // 5 + 1)
+        @pl.when(n == 3 + PAIRS + items // 2)
         def _():
             to_y(1)
 
@@ -331,7 +331,9 @@
             c.wait_send()
 
 
-EVENTS = {1: (3, 4), 6: (5, 6), 9: (7,)}
+EVENTS = {0: (3,), 1: (4,), 3: (5,), 4: (6,), 6: (7,)}
+
+PAIRS = 4
 
 
 def build(dims, block, tile):
@@ -369,7 +371,7 @@
                 dma((2,)), dma((2,)), dma((ny,)), dma((ny,)), dma((2,)), dma((2,)), dma((3, most)), dma((3, most)),
             ],
             compiler_params=pltpu.CompilerParams(
-                collective_id=0, has_side_effects=True, vmem_limit_bytes=48 * 2**20
+                collective_id=0, has_side_effects=True, vmem_limit_bytes=60 * 2**20
             ),
             name="iteration",
         )(points.T, scales.reshape(1, DESIGN), solution.T, residual.T, direction.T)

time: 81.2 us -> 76.6 us (0.943)
  local copies, waits for them, and re-layouts: 5.61 us -> 2.82 us
  Pallas kernels: 74.6 us -> 72.9 us
    unnamed x13 -> x7, local copies, waits for them, and re-layouts: 5.61 us -> 2.82 us
    pallas_call x1, Pallas kernels: 74.6 us -> 72.9 us  [body(): pl.pallas_call(functools.partial(kernel, dims, block, tile), out_shape=(s...]
where the time goes in v3:
time: 76.6 us; the launch traced here: 76.3 us
  Pallas kernels  72.9 us (95%)
  local copies, waits for them, and re-layouts  2.82 us (4%)
    pallas_call x1, Pallas kernels, body(): pl.pallas_call(functools.partial(kernel, dims, block, tile), out_shape=(s...  72.9 us
    unnamed x7, local copies, waits for them, and re-layouts  2.82 us

profile of v3, /device:TPU:1, one launch (start us, length us, event | category | flops | bytes accessed | tf_op | source)
XLA Modules:
  0.0 76.3 jit_solution(11197034432416955113)
XLA Ops:
  0.6 72.9 %iteration.1 = (f32[80,97]{1,0:T(8,128)}, f32[80,97]{1,0:T(8,128)}, f32[80,97]{1,0:T(8,128)}) custom-call(f32[80,96]{1,0:T(8,128)} %bitcast.8, f32[1,96]{1,0:T(1,128)} %bitcast.15, f32[80,97]{1,0:T(8,128)} %bitcast.9, f32[80,97]{1,0:T(8,128)} %bitcast.10, f32[80,97]{1,0:T(8,128)} %bitcast.11), custom_call_target="tpu_custom_call" | custom-call | tf_op jit(solution)/shard_map/iteration/pallas_call | solution.py:350
  73.5 0.0 copy-start.1
  73.5 1.4 %copy.11 = f32[97,80]{0,1:T(8,128)} copy(f32[97,80]{0,1:T(8,128)} %bitcast.14) | data formatting | bytes 62080
  74.9 0.0 copy-done.1
  74.9 0.0 copy-start
  74.9 0.6 copy.12
  75.5 0.2 copy-done
  75.7 0.6 copy.13
Async XLA Ops:
  73.5 1.4 %copy-start.1 = (f32[80,97]{1,0:T(8,128)S(1)}, f32[80,97]{1,0:T(8,128)}, u32[]{:S(2)}) copy-start(f32[80,97]{1,0:T(8,128)} %get-tuple-element.7) | copy-start | bytes 93124
  74.9 0.8 %copy-start = (f32[80,97]{1,0:T(8,128)S(1)}, f32[80,97]{1,0:T(8,128)}, u32[]{:S(2)}) copy-start(f32[80,97]{1,0:T(8,128)} %get-tuple-element.8) | copy-start | bytes 93124

commit v4 on v3

--- a/solution.py
+++ b/solution.py
@@ -46,9 +46,9 @@
 
 def kernel(
     dims, block, tile,
-    points_hbm, scales_hbm, solution_hbm, residual_hbm, direction_hbm,
-    solution_out, residual_out, direction_out,
-    points_ref, scales_ref, solution_ref, residual_ref, direction_ref,
+    points_hbm, scales_hbm, residual_hbm, direction_hbm,
+    image_out, sums_out,
+    points_ref, scales_ref, residual_ref, direction_ref,
     pad, rows, cols, stream, coord_hi, coord_lo, slope_hi, slope_lo, grad_hi, grad_lo, pipe, acc,
     part, from_core, whole, from_y, vec, vec_in,
     load, z_send, z_recv, x_send, x_recv, y_send, y_recv, c_send, c_recv,
@@ -77,7 +77,7 @@
 
     inputs = [
         (points_hbm, points_ref), (scales_hbm, scales_ref), (direction_hbm, direction_ref),
-        (residual_hbm, residual_ref), (solution_hbm, solution_ref),
+        (residual_hbm, residual_ref),
     ]
     loads = [pltpu.make_async_copy(src, dst, load.at[i]) for i, (src, dst) in enumerate(inputs)]
     for c in loads:
@@ -284,6 +284,7 @@
         total = total + from_y[r]
     image = jnp.where(lane == 0, total, (total - own_row * total[:, 0:1]) * (1.0 / ROOT))[:, 0 : DESIGN + 1]
 
+    image_out[...] = image
     sums = [norm_old, total_of(direction * image), total_of(residual * image), total_of(image * image)]
     spot = lax.broadcasted_iota(jnp.int32, (1, LANES), 1)
     line = jnp.zeros((1, LANES), F32)
@@ -307,13 +308,7 @@
             c.wait_recv()
             line = line + vec_in[s, i]
 
-    norm_old, curvature, cross, square = (line[:, k : k + 1] for k in range(4))
-    step_size = norm_old / curvature
-    norm_new = norm_old - 2.0 * step_size * cross + step_size * step_size * square
-    residual_next = residual - step_size * image
-    solution_out[...] = solution_ref[...] + step_size * direction
-    residual_out[...] = residual_next
-    direction_out[...] = residual_next + norm_new / norm_old * direction
+    sums_out[...] = line
 
     for r in range(1, nz):
         z_gather(r).wait_send()
@@ -331,6 +326,33 @@
             c.wait_send()
 
 
+def finish(
+    image_ref, sums_ref, solution_hbm, residual_hbm, direction_hbm,
+    solution_out, residual_out, direction_out, given, made, load, store,
+):
+    inputs, outputs = (solution_hbm, residual_hbm, direction_hbm), (solution_out, residual_out, direction_out)
+    loads = [pltpu.make_async_copy(src, given.at[i], load.at[i]) for i, src in enumerate(inputs)]
+    stores = [pltpu.make_async_copy(made.at[i], dst, store.at[i]) for i, dst in enumerate(outputs)]
+    for c in loads:
+        c.start()
+    norm_old, curvature, cross, square = (sums_ref[:, k : k + 1] for k in range(4))
+    step_size = norm_old / curvature
+    norm_new = norm_old - 2.0 * step_size * cross + step_size * step_size * square
+    ratio = norm_new / norm_old
+    for c in loads:
+        c.wait()
+    direction = given[2]
+    made[0] = given[0] + step_size * direction
+    stores[0].start()
+    residual_next = given[1] - step_size * image_ref[...]
+    made[1] = residual_next
+    stores[1].start()
+    made[2] = residual_next + ratio * direction
+    stores[2].start()
+    for c in stores:
+        c.wait()
+
+
 EVENTS = {0: (3,), 1: (4,), 3: (5,), 4: (6,), 6: (7,)}
 
 PAIRS = 4
@@ -344,14 +366,14 @@
     dma = pltpu.SemaphoreType.DMA
     vmem, hbm = pl.BlockSpec(memory_space=pltpu.VMEM), pl.BlockSpec(memory_space=pltpu.HBM)
     state = jax.ShapeDtypeStruct((block, DESIGN + 1), F32)
-    inputs = [(block, DESIGN), (1, DESIGN)] + [(block, DESIGN + 1)] * 3
+    inputs = [(block, DESIGN), (1, DESIGN)] + [(block, DESIGN + 1)] * 2
 
     def body(points, scales, solution, residual, direction):
-        outs = pl.pallas_call(
+        image, sums = pl.pallas_call(
             functools.partial(kernel, dims, block, tile),
-            out_shape=(state, state, state),
-            in_specs=[hbm] * 5,
-            out_specs=(vmem, vmem, vmem),
+            out_shape=(state, jax.ShapeDtypeStruct((1, LANES), F32)),
+            in_specs=[hbm] * 4,
+            out_specs=(vmem, vmem),
             scratch_shapes=[
                 *[pltpu.VMEM(shape, F32) for shape in inputs],
                 pltpu.VMEM((2, block, LANES), F32),
@@ -367,14 +389,25 @@
                 pltpu.VMEM((ny, block, LANES), F32),
                 pltpu.VMEM((3, 1, LANES), F32),
                 pltpu.VMEM((3, most, 1, LANES), F32),
-                dma((5,)), dma((nz,)), dma((nz,)), dma((nz * nx,)), dma((nz * nx,)), dma((ny,)), dma((ny,)),
+                dma((4,)), dma((nz,)), dma((nz,)), dma((nz * nx,)), dma((nz * nx,)), dma((ny,)), dma((ny,)),
                 dma((2,)), dma((2,)), dma((ny,)), dma((ny,)), dma((2,)), dma((2,)), dma((3, most)), dma((3, most)),
             ],
             compiler_params=pltpu.CompilerParams(
                 collective_id=0, has_side_effects=True, vmem_limit_bytes=60 * 2**20
             ),
             name="iteration",
-        )(points.T, scales.reshape(1, DESIGN), solution.T, residual.T, direction.T)
+        )(points.T, scales.reshape(1, DESIGN), residual.T, direction.T)
+        outs = pl.pallas_call(
+            finish,
+            out_shape=(state, state, state),
+            in_specs=[vmem, vmem, hbm, hbm, hbm],
+            out_specs=(hbm, hbm, hbm),
+            scratch_shapes=[
+                pltpu.VMEM((3, block, DESIGN + 1), F32), pltpu.VMEM((3, block, DESIGN + 1), F32), dma((3,)), dma((3,)),
+            ],
+            compiler_params=pltpu.CompilerParams(vmem_limit_bytes=60 * 2**20),
+            name="update",
+        )(image, sums, solution.T, residual.T, direction.T)
         return tuple(o.T for o in outs)
 
     return body

time: 76.6 us -> 76 us (level)
  local copies, waits for them, and re-layouts: 2.82 us -> 0 us
  Pallas kernels: 72.9 us -> 75.1 us
    unnamed x7 -> x0, local copies, waits for them, and re-layouts: 2.82 us -> none
    pallas_call x0 -> x1, Pallas kernels: none -> 2.37 us  [body(): pl.pallas_call(finish, out_shape=(state, state, state), in_specs=[vmem, v...]
where the time goes in v4:
time: 76 us; the launch traced here: 75.7 us
  Pallas kernels  75.1 us (99%)
    pallas_call x1, Pallas kernels, body(): pl.pallas_call(functools.partial(kernel, dims, block, tile), out_shape=(s...  72.7 us
    pallas_call x1, Pallas kernels, body(): pl.pallas_call(finish, out_shape=(state, state, state), in_specs=[vmem, v...  2.37 us

profile of v4, /device:TPU:1, one launch (start us, length us, event | category | flops | bytes accessed | tf_op | source)
XLA Modules:
  0.0 75.7 jit_solution(11729723709675031305)
XLA Ops:
  0.6 72.7 %iteration.1 = (f32[80,97]{1,0:T(8,128)}, f32[1,128]{1,0:T(1,128)}) custom-call(f32[80,96]{1,0:T(8,128)} %bitcast.13, f32[1,96]{1,0:T(1,128)} %bitcast.14, f32[80,97]{1,0:T(8,128)} %bitcast.8, f32[80,97]{1,0:T(8,128)} %bitcast.10), custom_call_target="tpu_custom_call" | custom-call | tf_op jit(solution)/shard_map/iteration/pallas_call | solution.py:372
  73.3 2.4 %update.1 = (f32[80,97]{1,0:T(8,128)}, f32[80,97]{1,0:T(8,128)}, f32[80,97]{1,0:T(8,128)}) custom-call(f32[80,97]{1,0:T(8,128)} %get-tuple-element.8.image_ref, f32[1,128]{1,0:T(1,128)} %get-tuple-element.9.sums_ref, f32[80,97]{1,0:T(8,128)} %bitcast.12, f32[80,97]{1,0:T(8,128)} %bitcast.9, f32[80,97]{1,0:T(8,128)} %bitcast.11), custom_call_target="tpu_custom_call" | custom-call | tf_op jit(solution)/shard_map/update/pallas_call | solution.py:400

commit v5 on v4

--- a/solution.py
+++ b/solution.py
@@ -143,13 +143,15 @@
         for i in range(1, nx):
             x_gather(r, i).start()
 
-    for r in range(1, max(ny, nz)):
-        if r < ny:
-            y_gather(r).start()
-        if r < nz:
-            z_gather(r).start()
-        if r == 1:
-            pass_on(0)
+    for r in range(1, per):
+        y_gather(r).start()
+    for r in range(1, min(nz, 3)):
+        z_gather(r).start()
+    pass_on(0)
+    for r in range(3, nz):
+        z_gather(r).start()
+    for r in range(per, ny):
+        y_gather(r).start()
     acc[...] = jnp.zeros_like(acc)
     for c in loads[3:]:
         c.wait()
@@ -292,8 +294,8 @@
         line = jnp.where(spot == k, value, line)
 
     stages = [
+        [at_cx(c, d) for c in range(nc) for d in range(nx) if c or d],
         [at_z(d) for d in range(1, nz)],
-        [at_cx(c, d) for c in range(nc) for d in range(nx) if c or d],
         [at_y(d) for d in range(1, ny)],
     ]
     exchanges = [

time: 76 us -> 75.5 us (level)
  Pallas kernels: 75.1 us -> 74.2 us
    pallas_call x1, Pallas kernels: 72.7 us -> 71.8 us  [body(): pl.pallas_call(functools.partial(kernel, dims, block, tile), out_shape=(s...]
where the time goes in v5:
time: 75.5 us; the launch traced here: 74.8 us
  Pallas kernels  74.2 us (98%)
    pallas_call x1, Pallas kernels, body(): pl.pallas_call(functools.partial(kernel, dims, block, tile), out_shape=(s...  71.8 us
    pallas_call x1, Pallas kernels, body(): pl.pallas_call(finish, out_shape=(state, state, state), in_specs=[vmem, v...  2.37 us

profile of v5, /device:TPU:1, one launch (start us, length us, event | category | flops | bytes accessed | tf_op | source)
XLA Modules:
  0.0 74.8 jit_solution(15466464000110570046)
XLA Ops:
  0.6 71.8 %iteration.1 = (f32[80,97]{1,0:T(8,128)}, f32[1,128]{1,0:T(1,128)}) custom-call(f32[80,96]{1,0:T(8,128)} %bitcast.13, f32[1,96]{1,0:T(1,128)} %bitcast.14, f32[80,97]{1,0:T(8,128)} %bitcast.8, f32[80,97]{1,0:T(8,128)} %bitcast.10), custom_call_target="tpu_custom_call" | custom-call | tf_op jit(solution)/shard_map/iteration/pallas_call | solution.py:374
  72.5 2.4 %update.1 = (f32[80,97]{1,0:T(8,128)}, f32[80,97]{1,0:T(8,128)}, f32[80,97]{1,0:T(8,128)}) custom-call(f32[80,97]{1,0:T(8,128)} %get-tuple-element.8.image_ref, f32[1,128]{1,0:T(1,128)} %get-tuple-element.9.sums_ref, f32[80,97]{1,0:T(8,128)} %bitcast.12, f32[80,97]{1,0:T(8,128)} %bitcast.9, f32[80,97]{1,0:T(8,128)} %bitcast.11), custom_call_target="tpu_custom_call" | custom-call | tf_op jit(solution)/shard_map/update/pallas_call | solution.py:402
